TPU v7x, 1024 devices: a whole 8x8x8 slice. The times are simulated.
1024 devices in a mesh: kgrp: 16 (over x, z_hi), row: 8 (over z_lo, core), col: 8 (over y).
Axes of the slice: x: 8, y: 8, z: 8 (z_hi: 2, z_lo: 4; z = z_hi * 4 + z_lo), core: 2. Of those that a mesh axis runs over, the one named last changes fastest.
Arguments:
- occ_orbitals: bfloat16 [32, 1024, 2, 512], P('kgrp', ('row', 'col')), may hold values from -5 to 5
- emp_orbitals: bfloat16 [32, 1024, 2, 512], P('kgrp', ('row', 'col')), may hold values from -5 to 5
- energies: float32 [2, 32, 512], replicated, may hold values from 0.05 to 1.5
- band_order: int32 [2, 32, 512], replicated, may hold values from 0 to 511, each once within a row
- imag_times: float32 [2], replicated, may hold values from 0.3 to 3
- kq_map: int32 [2, 32], replicated, may hold values from 0 to 31, each once within a row
- slot_kpoint: int32 [32], replicated, may hold values from 0 to 31, each once
Outputs:
- suscept: float32 [2, 2, 8, 128, 2, 1024], P(None, None, 'col', 'kgrp', None, 'row')
Inputs may be any that keep to these rules, and one draw needn't show every extreme that they name: `kq_map`: each row is a permutation of the k-point ids. `slot_kpoint`: a permutation of the k-point ids. `band_order`: each row over the last dimension is a permutation of the ranks.
All inputs are finite; a program needn't handle non-finite values.
Results may differ from a plain program's by a relative error of at most 0.0003.
Values may be sent and summed in bfloat16 or wider, within the bound.
A program may use at most 32 MiB of HBM per device.

v0:
```python
import jax
import jax.numpy as jnp
from jax import lax
from jax.sharding import PartitionSpec as P


def joined_along(blocks, dim):
    shape = list(blocks.shape[1:])
    shape[dim] *= blocks.shape[0]
    return jnp.moveaxis(blocks, 0, dim).reshape(shape)


def sent_to_all(value, axis):
    peers = lax.axis_size(axis)
    return lax.all_to_all(
        jnp.broadcast_to(value[None], (peers, *value.shape)), axis, 0, 0, tiled=True
    )


def gather_directly(value, axis, dim):
    return joined_along(sent_to_all(value, axis), dim)


def cut_along(value, dim, peers):
    shape = value.shape
    blocks = value.reshape(*shape[:dim], peers, shape[dim] // peers, *shape[dim + 1 :])
    return jnp.moveaxis(blocks, dim, 0)


def summed_on_arrival(value, axis, dim):
    blocks = cut_along(value, dim, lax.axis_size(axis))
    arrived = lax.all_to_all(blocks, axis, split_axis=0, concat_axis=0, tiled=True)
    return arrived.sum(axis=0)


def table_row(lookup_table, wanted):
    positions = jnp.arange(lookup_table.shape[0], dtype=jnp.int32)
    chosen = positions[:, None] == wanted
    return jnp.sum(jnp.where(chosen, lookup_table, jnp.zeros_like(lookup_table)), axis=0)


def band_weights(levels, band_rank, imag_times):
    picked = jnp.take(levels, band_rank, axis=0)
    return jnp.exp(-picked[None, :] * imag_times[:, None])


def green_tile(row_panel, col_panel, weights):
    times_count = weights.shape[0]
    scaled = (row_panel[None] * weights[:, None, None, :]).astype(jnp.bfloat16)
    scaled = scaled.reshape(times_count, row_panel.shape[0], -1)
    turned = jnp.concatenate([-col_panel[:, 1], col_panel[:, 0]], axis=1)
    stacked = jnp.concatenate([col_panel.reshape(col_panel.shape[0], -1), turned], axis=0)
    result = lax.dot_general(
        stacked, scaled, (((1,), (2,)), ((), ())), preferred_element_type=jnp.float32
    )
    return result.reshape(2, col_panel.shape[0], times_count, row_panel.shape[0])


def pair_term(held_tile, moved_tile, factor):
    real_part = held_tile[0] * moved_tile[0] + held_tile[1] * moved_tile[1]
    imag_part = held_tile[1] * moved_tile[0] - held_tile[0] * moved_tile[1]
    return factor * jnp.stack([real_part, imag_part])


def source_slots(kq_map, slot_kpoint, own_slots):
    positions = jnp.arange(slot_kpoint.shape[0], dtype=jnp.int32)
    own_kpoint = jnp.sum(
        jnp.where(own_slots[:, None] == positions[None, :], slot_kpoint[None, :], 0), axis=1
    )
    target = jnp.sum(
        jnp.where(own_kpoint[None, :, None] == positions[None, None, :], kq_map[:, None, :], 0),
        axis=2,
    )
    return jnp.sum(
        jnp.where(target[:, :, None] == slot_kpoint[None, None, :], positions[None, None, :], 0),
        axis=2,
    )


def shards(occ_orbitals, emp_orbitals, energies, band_order, imag_times, kq_map, slot_kpoint):
    groups = lax.axis_size("kgrp")
    per_group = occ_orbitals.shape[0]
    kpoints = groups * per_group
    transfers = kq_map.shape[0]
    factor = -1.0 / kpoints
    own_slots = lax.axis_index("kgrp") * per_group + jnp.arange(per_group, dtype=jnp.int32)
    sources = source_slots(kq_map, slot_kpoint, own_slots)
    flat_sources = sources.reshape(-1)
    initial = jnp.zeros((flat_sources.shape[0],) + emp_orbitals.shape[1:], jnp.float32)
    block_part = gather_directly(emp_orbitals, "kgrp", 0)
    numbered = block_part.shape[0]
    matches = (flat_sources[:, None] == jnp.arange(numbered, dtype=jnp.int32)[None, :]).astype(
        jnp.bfloat16
    )
    update = jnp.dot(matches, block_part.reshape(numbered, -1), preferred_element_type=jnp.float32)
    fetched = update.reshape(initial.shape).astype(jnp.bfloat16)
    occ_rows = gather_directly(occ_orbitals, "col", 1)
    occ_cols = gather_directly(occ_orbitals, "row", 1)
    tiles = []
    for position in range(per_group):
        weights = band_weights(
            table_row(energies[0], own_slots[position]),
            table_row(band_order[0], own_slots[position]),
            imag_times,
        )
        tiles.append(green_tile(occ_rows[position], occ_cols[position], weights))
    emp_rows = gather_directly(fetched, "col", 1)
    emp_cols = gather_directly(fetched, "row", 1)

    def transfer_terms(transfer):
        partial_value = None
        for position in range(per_group):
            source = sources[transfer, position]
            weights = band_weights(
                table_row(energies[1], source), table_row(band_order[1], source), imag_times
            )
            moved_index = transfer * per_group + position
            moved_tile = green_tile(emp_rows[moved_index], emp_cols[moved_index], weights)
            addition = pair_term(tiles[position], moved_tile, factor)
            partial_value = addition if partial_value is None else partial_value + addition
        return partial_value

    terms_all = jnp.stack([transfer_terms(transfer) for transfer in range(transfers)], axis=1)
    summed = summed_on_arrival(terms_all, "kgrp", 2)
    return summed[:, :, None]


def solution(mesh):
    in_specs = (
        P("kgrp", ("row", "col"), None, None),
        P("kgrp", ("row", "col"), None, None),
        P(),
        P(),
        P(),
        P(),
        P(),
    )
    out_specs = P(None, None, "col", "kgrp", None, "row")
    return jax.shard_map(shards, mesh=mesh, in_specs=in_specs, out_specs=out_specs, check_vma=False)
```

profile of v0, /device:TPU:16, one launch (start us, length us, event | category | flops | bytes accessed | tf_op | source)
XLA Modules:
  0.0 204.4 jit_solution(15012196175596648321)
XLA Ops:
  0.0 2.1 %broadcast_in_dim.171 = bf16[8,2,16,2,512]{4,3,2,1,0:T(2,128)(2,1)} broadcast(bf16[2,16,2,512]{3,2,1,0:T(2,128)(2,1)} %param.9), dimensions={1,2,3,4} | broadcast | bytes 589824 | tf_op jit(solution)/shard_map/broadcast_in_dim | solution.py:16
  2.1 10.1 %all-to-all-start = ((bf16[8,2,16,2,512]{4,3,2,1,0:T(2,128)(2,1)}), bf16[8,2,16,2,512]{4,3,2,1,0:T(2,128)(2,1)S(1)}, u32[]{:S(2)}, u32[]{:S(2)}) async-start(bf16[8,2,16,2,512]{4,3,2,1,0:T(2,128)(2,1)} %broadcast_in_dim.171), calls=%async_computation | async-start | bytes 1048576 | tf_op jit(solution)/shard_map/all_to_all | solution.py:15
  12.2 0.6 fusion.77
  12.8 0.2 fusion.66
  13.2 0.2 fusion.63
  13.4 0.7 fusion.76
  14.2 1.2 iota_compare_fusion.2
  15.4 1.2 iota_compare_fusion.4
  16.6 1.3 iota_compare_fusion.6
  18.3 3.5 %gather_fusion.5 = f32[512]{0:T(512)S(1)} fusion(f32[512]{0:T(512)S(1)} %get-tuple-element.13, s32[1024]{0:T(1024)S(1)} %pad_clamp_fusion), kind=kCustom, calls=%fused_computation.5.clone | custom fusion | bytes 6144 | tf_op jit(solution)/shard_map/jit(_take)/gather | solution.py:43
  21.8 5.7 %all-to-all-done = bf16[8,2,16,2,512]{4,3,2,1,0:T(2,128)(2,1)S(1)} async-done(((bf16[8,2,16,2,512]{4,3,2,1,0:T(2,128)(2,1)}), bf16[8,2,16,2,512]{4,3,2,1,0:T(2,128)(2,1)S(1)}, u32[]{:S(2)}, u32[]{:S(2)}) %all-to-all-start) | async-done | bytes 524320 | tf_op jit(solution)/shard_map/all_to_all | solution.py:15
  27.6 1.9 broadcast_in_dim.179
  29.5 16.2 %all-to-all-start.2 = ((bf16[16,2,16,2,512]{4,3,2,1,0:T(2,128)(2,1)}), bf16[16,2,16,2,512]{4,3,2,1,0:T(2,128)(2,1)S(1)}, u32[]{:S(2)}, u32[]{:S(2)}) async-start(bf16[16,2,16,2,512]{4,3,2,1,0:T(2,128)(2,1)} %broadcast_in_dim.179), calls=%async_computation.2 | async-start | bytes 2097152 | tf_op jit(solution)/shard_map/all_to_all | solution.py:15
  45.8 3.5 %gather_fusion.4 = f32[512]{0:T(512)S(1)} fusion(f32[512]{0:T(512)S(1)} %get-tuple-element.14, s32[1024]{0:T(1024)S(1)} %pad_clamp_fusion.1), kind=kCustom, calls=%fused_computation.4.clone | custom fusion | bytes 6144 | tf_op jit(solution)/shard_map/jit(_take)/gather | solution.py:43
  49.3 3.5 %gather_fusion.3 = f32[512]{0:T(512)S(1)} fusion(f32[512]{0:T(512)S(1)} %get-tuple-element.15, s32[1024]{0:T(1024)S(1)} %pad_clamp_fusion.2), kind=kCustom, calls=%fused_computation.3.clone | custom fusion | bytes 6144 | tf_op jit(solution)/shard_map/jit(_take)/gather | solution.py:43
  52.8 3.5 %gather_fusion.2 = f32[512]{0:T(512)S(1)} fusion(f32[512]{0:T(512)S(1)} %get-tuple-element.16, s32[1024]{0:T(1024)S(1)} %pad_clamp_fusion.3), kind=kCustom, calls=%fused_computation.2.clone | custom fusion | bytes 6144 | tf_op jit(solution)/shard_map/jit(_take)/gather | solution.py:43
  56.4 3.5 %gather_fusion.1 = f32[512]{0:T(512)S(1)} fusion(f32[512]{0:T(512)S(1)} %get-tuple-element.12, s32[1024]{0:T(1024)S(1)} %pad_clamp_fusion.4), kind=kCustom, calls=%fused_computation.1.clone | custom fusion | bytes 6144 | tf_op jit(solution)/shard_map/jit(_take)/gather | solution.py:43
  59.9 22.6 %all-to-all-done.2 = bf16[16,2,16,2,512]{4,3,2,1,0:T(2,128)(2,1)S(1)} async-done(((bf16[16,2,16,2,512]{4,3,2,1,0:T(2,128)(2,1)}), bf16[16,2,16,2,512]{4,3,2,1,0:T(2,128)(2,1)S(1)}, u32[]{:S(2)}, u32[]{:S(2)}) %all-to-all-start.2) | async-done | bytes 1048608 | tf_op jit(solution)/shard_map/all_to_all | solution.py:15
  82.4 7.9 %all-to-all-start.1 = ((bf16[8,2,16,2,512]{4,3,2,1,0:T(2,128)(2,1)}), bf16[8,2,16,2,512]{4,3,2,1,0:T(2,128)(2,1)S(1)}, u32[]{:S(2)}, u32[]{:S(2)}) async-start(bf16[8,2,16,2,512]{4,3,2,1,0:T(2,128)(2,1)} %broadcast_in_dim.171), calls=%async_computation.1 | async-start | bytes 1048576 | tf_op jit(solution)/shard_map/all_to_all | solution.py:15
  90.4 0.8 reshape_reshape.3
  91.2 0.8 dot_general.27
  92.0 0.7 convolution_convert_fusion
  92.8 11.2 %all-to-all-done.1 = bf16[8,2,16,2,512]{4,3,2,1,0:T(2,128)(2,1)S(1)} async-done(((bf16[8,2,16,2,512]{4,3,2,1,0:T(2,128)(2,1)}), bf16[8,2,16,2,512]{4,3,2,1,0:T(2,128)(2,1)S(1)}, u32[]{:S(2)}, u32[]{:S(2)}) %all-to-all-start.1) | async-done | bytes 524320 | tf_op jit(solution)/shard_map/all_to_all | solution.py:15
  103.9 1.9 broadcast_in_dim.180
  105.9 3.6 %all-to-all-start.3 = ((bf16[8,4,16,2,512]{4,3,2,1,0:T(2,128)(2,1)}), bf16[8,4,16,2,512]{4,3,2,1,0:T(2,128)(2,1)S(1)}, u32[]{:S(2)}, u32[]{:S(2)}) async-start(bf16[8,4,16,2,512]{4,3,2,1,0:T(2,128)(2,1)} %broadcast_in_dim.180), calls=%async_computation.3 | async-start | bytes 2097152 | tf_op jit(solution)/shard_map/all_to_all | solution.py:15
  109.5 3.5 %gather_fusion = f32[512]{0:T(512)S(1)} fusion(f32[512]{0:T(512)S(1)} %get-tuple-element.17, s32[1024]{0:T(1024)S(1)} %pad_clamp_fusion.5), kind=kCustom, calls=%fused_computation.clone | custom fusion | bytes 6144 | tf_op jit(solution)/shard_map/jit(_take)/gather | solution.py:43
  113.0 0.6 copy-done.8
  113.7 0.6 copy.83
  114.3 0.6 copy.77
  115.0 20.9 %all-to-all-done.3 = bf16[8,4,16,2,512]{4,3,2,1,0:T(2,128)(2,1)S(1)} async-done(((bf16[8,4,16,2,512]{4,3,2,1,0:T(2,128)(2,1)}), bf16[8,4,16,2,512]{4,3,2,1,0:T(2,128)(2,1)S(1)}, u32[]{:S(2)}, u32[]{:S(2)}) %all-to-all-start.3) | async-done | bytes 1048608 | tf_op jit(solution)/shard_map/all_to_all | solution.py:15
  136.0 4.9 %all-to-all-start.4 = ((bf16[8,4,16,2,512]{4,3,2,1,0:T(2,128)(2,1)}), bf16[8,4,16,2,512]{4,3,2,1,0:T(2,128)(2,1)S(1)}, u32[]{:S(2)}, u32[]{:S(2)}) async-start(bf16[8,4,16,2,512]{4,3,2,1,0:T(2,128)(2,1)} %broadcast_in_dim.180), calls=%async_computation.4 | async-start | bytes 2097152 | tf_op jit(solution)/shard_map/all_to_all | solution.py:15
  140.9 0.4 fusion.75
  141.4 0.4 slice_convert_fusion.5
  142.1 0.3 fusion.3
  142.5 0.3 fusion.1
  142.8 1.2 fusion.74
  144.1 0.8 copy.81
  144.9 0.7 fusion.45
  145.6 22.7 %all-to-all-done.4 = bf16[8,4,16,2,512]{4,3,2,1,0:T(2,128)(2,1)S(1)} async-done(((bf16[8,4,16,2,512]{4,3,2,1,0:T(2,128)(2,1)}), bf16[8,4,16,2,512]{4,3,2,1,0:T(2,128)(2,1)S(1)}, u32[]{:S(2)}, u32[]{:S(2)}) %all-to-all-start.4) | async-done | bytes 1048608 | tf_op jit(solution)/shard_map/all_to_all | solution.py:15
  168.3 0.7 slice_convert_fusion.4
  169.8 0.8 copy-done
  170.6 0.3 fusion.6
  171.0 0.7 copy-done.5
  171.7 0.3 fusion.4
  172.1 0.3 fusion.5
  172.4 0.3 fusion.2
  173.0 30.7 %all_to_all.30 = f32[16,2,2,8,2,128]{5,3,4,2,1,0:T(8,128)S(1)} all-to-all(f32[16,2,2,8,2,128]{5,3,4,2,1,0:T(8,128)S(1)} %maximum_bitcast_fusion.12), channel_id=1, replica_groups=mesh['kgrp'=16,'row'=8,'col'=8] {'kgrp'}, dimensions={0} | all-to-all | bytes 1048576 | tf_op jit(solution)/shard_map/all_to_all | solution.py:32
  203.7 0.6 copy.59
  (81 shorter events, 2.2 us)
Async XLA Ops:
  2.1 10.8 %copy-start.9 = (s32[32]{0:T(128)S(1)}, s32[32]{0:T(128)}, u32[]{:S(2)}) copy-start(s32[32]{0:T(128)} %param.15) | copy-start | bytes 388
  2.1 11.0 %copy-start.7 = (s32[2,32]{1,0:T(2,128)S(1)}, s32[2,32]{1,0:T(2,128)}, u32[]{:S(2)}) copy-start(s32[2,32]{1,0:T(2,128)} %param.14) | copy-start | bytes 772
  2.1 15.9 %copy-start.1 = (s32[2,32,512]{2,1,0:T(8,128)S(1)}, s32[2,32,512]{2,1,0:T(8,128)}, u32[]{:S(2)}) copy-start(s32[2,32,512]{2,1,0:T(8,128)} %param.12) | copy-start | bytes 393220
  2.1 25.5 %all-to-all-start = ((bf16[8,2,16,2,512]{4,3,2,1,0:T(2,128)(2,1)}), bf16[8,2,16,2,512]{4,3,2,1,0:T(2,128)(2,1)S(1)}, u32[]{:S(2)}, u32[]{:S(2)}) async-start(bf16[8,2,16,2,512]{4,3,2,1,0:T(2,128)(2,1)} %broadcast_in_dim.171), calls=%async_computation | async-start | bytes 1048576 | tf_op jit(solution)/shard_map/all_to_all | solution.py:15
  12.2 6.0 %copy-start.2 = (f32[2,32,512]{2,1,0:T(8,128)S(1)}, f32[2,32,512]{2,1,0:T(8,128)}, u32[]{:S(2)}) copy-start(f32[2,32,512]{2,1,0:T(8,128)} %param.11) | copy-start | bytes 393220
  18.3 9.3 %copy-start.4 = (bf16[2,16,2,512]{3,2,1,0:T(2,128)(2,1)S(1)}, bf16[2,16,2,512]{3,2,1,0:T(2,128)(2,1)}, u32[]{:S(2)}) copy-start(bf16[2,16,2,512]{3,2,1,0:T(2,128)(2,1)} %param.10) | copy-start | bytes 196612
  29.5 53.0 %all-to-all-start.2 = ((bf16[16,2,16,2,512]{4,3,2,1,0:T(2,128)(2,1)}), bf16[16,2,16,2,512]{4,3,2,1,0:T(2,128)(2,1)S(1)}, u32[]{:S(2)}, u32[]{:S(2)}) async-start(bf16[16,2,16,2,512]{4,3,2,1,0:T(2,128)(2,1)} %broadcast_in_dim.179), calls=%async_computation.2 | async-start | bytes 2097152 | tf_op jit(solution)/shard_map/all_to_all | solution.py:15
  82.4 21.5 %all-to-all-start.1 = ((bf16[8,2,16,2,512]{4,3,2,1,0:T(2,128)(2,1)}), bf16[8,2,16,2,512]{4,3,2,1,0:T(2,128)(2,1)S(1)}, u32[]{:S(2)}, u32[]{:S(2)}) async-start(bf16[8,2,16,2,512]{4,3,2,1,0:T(2,128)(2,1)} %broadcast_in_dim.171), calls=%async_computation.1 | async-start | bytes 1048576 | tf_op jit(solution)/shard_map/all_to_all | solution.py:15
  105.9 30.1 %all-to-all-start.3 = ((bf16[8,4,16,2,512]{4,3,2,1,0:T(2,128)(2,1)}), bf16[8,4,16,2,512]{4,3,2,1,0:T(2,128)(2,1)S(1)}, u32[]{:S(2)}, u32[]{:S(2)}) async-start(bf16[8,4,16,2,512]{4,3,2,1,0:T(2,128)(2,1)} %broadcast_in_dim.180), calls=%async_computation.3 | async-start | bytes 2097152 | tf_op jit(solution)/shard_map/all_to_all | solution.py:15
  113.0 0.7 copy-start.8
  136.0 32.3 %all-to-all-start.4 = ((bf16[8,4,16,2,512]{4,3,2,1,0:T(2,128)(2,1)}), bf16[8,4,16,2,512]{4,3,2,1,0:T(2,128)(2,1)S(1)}, u32[]{:S(2)}, u32[]{:S(2)}) async-start(bf16[8,4,16,2,512]{4,3,2,1,0:T(2,128)(2,1)} %broadcast_in_dim.180), calls=%async_computation.4 | async-start | bytes 2097152 | tf_op jit(solution)/shard_map/all_to_all | solution.py:15
  169.6 1.0 copy-start
  169.7 1.0 copy-start.3
  169.8 0.9 copy-start.6
  171.0 0.7 copy-start.5
where the time goes:
time: 205 us; the launch traced here: 204 us
  waiting for transfers between devices  83.1 us (41%)
  starting transfers between devices  42.7 us (21%)
  local copies, waits for them, and re-layouts  37.3 us (18%)
  blocking collectives  30.7 us (15%)
  other arithmetic  7.06 us (3%)
  matrix products  2.73 us (1%)
    all_to_all x5, waiting for transfers between devices, sent_to_all(): lax.all_to_all(jnp.broadcast_to(value[None], (peers, *value.shape)), axis...  83.1 us
    all_to_all x5, starting transfers between devices, sent_to_all(): lax.all_to_all(jnp.broadcast_to(value[None], (peers, *value.shape)), axis...  42.7 us
    all_to_all x1, blocking collectives, summed_on_arrival(): lax.all_to_all(blocks, axis, split_axis=0, concat_axis=0, tiled=True)  30.7 us
    gather x6, local copies, waits for them, and re-layouts, band_weights(): picked = jnp.take(levels, band_rank, axis=0)  20.9 us
    broadcast_in_dim x3, local copies, waits for them, and re-layouts, sent_to_all(): jnp.broadcast_to(value[None], (peers, *value.shape))  5.94 us
    unnamed x44, local copies, waits for them, and re-layouts  4.94 us
  transfers between devices with their start and end apart: 5, of which 5 were waited for; matrix products, arithmetic and copies ran while one was open for 17% of the time, Pallas kernels for 0%

commit v1 on v0

v1 whole, which is shorter than its diff:
```python
import functools

import jax
import jax.numpy as jnp
from jax import lax
from jax.experimental import pallas as pl
from jax.experimental.pallas import tpu as pltpu
from jax.sharding import PartitionSpec as P

MESH = pl.DeviceIdType.MESH
CORES = 2
NEAR = (2, -2, 1, -1)


def band_weights(energies, band_order, imag_times, slots):
    levels = jnp.concatenate([energies[s, pl.ds(j, 1)] for s, j in slots], axis=0)
    ranks = jnp.concatenate([band_order[s, pl.ds(j, 1)] for s, j in slots], axis=0)
    levels = jnp.concatenate([levels, levels], axis=0)
    ranks = jnp.concatenate([ranks, ranks], axis=0)
    bands = levels.shape[1]
    picked = []
    for b in range(bands // 128):
        rank = ranks[:, b * 128 : (b + 1) * 128]
        lane = rank % 128
        found = jnp.zeros(rank.shape, jnp.float32)
        for c in range(bands // 128):
            taken = jnp.take_along_axis(levels[:, c * 128 : (c + 1) * 128], lane, axis=1)
            found = jnp.where(rank // 128 == c, taken, found)
        picked.append(found)
    picked = jnp.concatenate(picked, axis=1)
    return [jnp.exp(-picked * imag_times[t]) for t in range(2)]


def kernel(
    sizes,
    own_ref,
    energies,
    band_order,
    imag_times,
    kq_map,
    slot_kpoint,
    out_ref,
    rows,
    cols,
    packed,
    landed,
    inverse,
    row_send,
    row_recv,
    col_send,
    col_recv,
    mate_send,
    mate_recv,
    tile_send,
    tile_recv,
    local_sem,
):
    groups, row_count, col_count = sizes
    xs, line = groups // 2, row_count // CORES
    per_group = own_ref.shape[1]
    kpoints = groups * per_group
    group, row, y = lax.axis_index("kgrp"), lax.axis_index("row"), lax.axis_index("col")
    x, zh = group // 2, group % 2
    zl, core = row // CORES, row % CORES

    def along_y(step):
        return (group, row, lax.rem(y + step + col_count, col_count))

    def along_z(step):
        return (group, lax.rem(zl + step, line) * CORES + core, y)

    mate = (group, zl * CORES + 1 - core, y)
    others = [(dx, dz) for dx in (4, 3, 5, 2, 6, 1, 7, 0) for dz in (1, 0) if dx or dz]

    def group_at(dx, dz):
        return lax.rem(x + dx, xs) * 2 + lax.rem(zh + dz, 2)

    peers = [along_y(s) for s in NEAR] + [along_z(e) for e in range(1, line)] + [mate]
    peers += [(group_at(dx, dz), row, y) for dx, dz in others]
    barrier = pltpu.get_barrier_semaphore()
    for peer in peers:
        pl.semaphore_signal(barrier, inc=1, device_id=peer, device_id_type=MESH)

    mine = []
    for kind in range(2):
        for i, target in enumerate((rows.at[kind, y], cols.at[kind, row])):
            mine.append(
                pltpu.make_async_copy(own_ref.at[kind], target, local_sem.at[kind * 2 + i])
            )
    for copy in mine:
        copy.start()
    slots = [(s, group * per_group + p) for s in range(2) for p in range(per_group)]
    weights = band_weights(energies, band_order, imag_times, slots)

    def find(k, carry):
        total = jnp.int32(0)
        for s in range(kpoints):
            total = jnp.where(slot_kpoint[s] == k, s, total)
        inverse[k] = total
        return carry

    pl.semaphore_wait(barrier, len(peers))

    row_copies, col_copies, mate_copies, tile_copies = {}, {}, {}, {}

    def send_rows(kind, distance, step):
        source = lax.rem(y - (distance - step) + col_count, col_count)
        key = (kind, distance % col_count)
        held = own_ref.at[kind] if distance == step else rows.at[kind, source]
        row_copies[key] = pltpu.make_async_remote_copy(
            src_ref=held,
            dst_ref=rows.at[kind, source],
            send_sem=row_send.at[key[0], key[1]],
            recv_sem=row_recv.at[key[0], key[1]],
            device_id=along_y(step),
            device_id_type=MESH,
        )
        row_copies[key].start()

    def send_cols(kind, step):
        col_copies[kind, step] = pltpu.make_async_remote_copy(
            src_ref=own_ref.at[kind],
            dst_ref=cols.at[kind, row],
            send_sem=col_send.at[kind, step],
            recv_sem=col_recv.at[kind, step],
            device_id=along_z(step),
            device_id_type=MESH,
        )
        col_copies[kind, step].start()

    def send_mate(kind, step):
        source = lax.rem(zl - step + line, line) * CORES + core
        mate_copies[kind, step] = pltpu.make_async_remote_copy(
            src_ref=cols.at[kind, source] if step else own_ref.at[kind],
            dst_ref=cols.at[kind, source],
            send_sem=mate_send.at[kind, step],
            recv_sem=mate_recv.at[kind, step],
            device_id=mate,
            device_id_type=MESH,
        )
        mate_copies[kind, step].start()

    for kind in range(2):
        for step in NEAR[:2]:
            send_rows(kind, step, step)
        for step in (2, 3, 1):
            send_cols(kind, step)
        for step in NEAR[2:]:
            send_rows(kind, step, step)
        send_mate(kind, 0)
    lax.fori_loop(0, kpoints, find, 0)
    for kind in range(2):
        for sign in (1, -1):
            row_copies[kind, 2 * sign % col_count].wait_recv()
            if (sign == 1) == (kind == 0):
                send_rows(kind, 4 * sign, 2 * sign)
            send_rows(kind, 3 * sign, sign)
        for step in (1, 2, 3):
            col_copies[kind, step].wait_recv()
            send_mate(kind, step)

    for copy in mine:
        copy.wait()
    for kind in range(2):
        for distance in (1, 7, 3, 5, 4):
            row_copies[kind, distance].wait_recv()
        for step in range(line):
            mate_copies[kind, step].wait_recv()
        for slot in range(per_group):
            panel = rows[kind, :, slot].reshape(-1, own_ref.shape[-1])
            others_panel = cols[kind, :, slot].reshape(-1, own_ref.shape[-1])
            bands = panel.shape[1] // 2
            w = [weights[t][kind * per_group + slot : kind * per_group + slot + 1] for t in range(2)]
            wide = panel.astype(jnp.float32)
            scaled = jnp.concatenate(
                [wide * jnp.concatenate([w[t], w[t]], axis=1) for t in range(2)], axis=0
            ).astype(jnp.bfloat16)
            turned = jnp.concatenate([-others_panel[:, bands:], others_panel[:, :bands]], axis=1)
            stacked = jnp.concatenate([others_panel, turned], axis=0)
            tile = lax.dot_general(
                stacked, scaled, (((1,), (1,)), ((), ())), preferred_element_type=jnp.float32
            )
            count = panel.shape[0]
            for comp in range(2):
                for t in range(2):
                    part = tile[comp * count : (comp + 1) * count, t * count : (t + 1) * count]
                    packed[kind, :, slot, comp, t] = part.reshape(groups, -1, count)
        for n, (dx, dz) in enumerate(others):
            there = group_at(dx, dz)
            tile_copies[kind, n] = pltpu.make_async_remote_copy(
                src_ref=packed.at[kind, there],
                dst_ref=landed.at[kind, pl.ds(group * per_group, per_group)],
                send_sem=tile_send.at[kind, n],
                recv_sem=tile_recv.at[kind, n],
                device_id=(there, row, y),
                device_id_type=MESH,
            )
            tile_copies[kind, n].start()
        landed[kind, pl.ds(group * per_group, per_group)] = packed[kind, group]

    for copy in (*row_copies.values(), *col_copies.values(), *mate_copies.values()):
        copy.wait_send()
    for copy in tile_copies.values():
        copy.wait_recv()

    def add(j, totals):
        held_re, held_im = landed[0, j, 0], landed[0, j, 1]
        kpoint = slot_kpoint[j]
        new = []
        for q in range(2):
            source = inverse[kq_map[q, kpoint]]
            moved_re, moved_im = landed[1, source, 0], landed[1, source, 1]
            new.append(totals[2 * q] + (held_re * moved_re + held_im * moved_im))
            new.append(totals[2 * q + 1] + (held_im * moved_re - held_re * moved_im))
        return tuple(new)

    zero = jnp.zeros(landed.shape[3:], jnp.float32)
    totals = lax.fori_loop(0, kpoints, add, (zero,) * 4)
    for q in range(2):
        for comp in range(2):
            out_ref[comp, q] = totals[2 * q + comp] * (-1.0 / kpoints)
    for copy in tile_copies.values():
        copy.wait_send()


def shards(sizes, occ, emp, energies, band_order, imag_times, kq_map, slot_kpoint):
    groups, row_count, col_count = sizes
    per_group, chunk = occ.shape[:2]
    width = occ.shape[2] * occ.shape[3]
    points = row_count * chunk
    share = points // groups
    own = jnp.stack([occ, emp]).reshape(2, per_group, chunk, width)
    vmem, smem = pl.BlockSpec(memory_space=pltpu.VMEM), pl.BlockSpec(memory_space=pltpu.SMEM)
    dma = pltpu.SemaphoreType.DMA
    result = pl.pallas_call(
        functools.partial(kernel, sizes),
        out_shape=jax.ShapeDtypeStruct((2, 2, 2, share, points), jnp.float32),
        in_specs=[vmem, vmem, vmem, smem, smem, smem],
        out_specs=vmem,
        scratch_shapes=[
            pltpu.VMEM((2, col_count, per_group, chunk, width), jnp.bfloat16),
            pltpu.VMEM((2, row_count, per_group, chunk, width), jnp.bfloat16),
            pltpu.VMEM((2, groups, per_group, 2, 2, share, points), jnp.float32),
            pltpu.VMEM((2, groups * per_group, 2, 2, share, points), jnp.float32),
            pltpu.SMEM((groups * per_group,), jnp.int32),
            dma((2, col_count)),
            dma((2, col_count)),
            dma((2, 4)),
            dma((2, 4)),
            dma((2, 4)),
            dma((2, 4)),
            dma((2, 16)),
            dma((2, 16)),
            dma((4,)),
        ],
        compiler_params=pltpu.CompilerParams(collective_id=0, has_side_effects=True),
        name="polarizability",
    )(own, energies, band_order, imag_times, kq_map, slot_kpoint)
    return jnp.transpose(result, (0, 1, 3, 2, 4))[:, :, None]


def solution(mesh):
    sizes = (mesh.shape["kgrp"], mesh.shape["row"], mesh.shape["col"])
    in_specs = (
        P("kgrp", ("row", "col"), None, None),
        P("kgrp", ("row", "col"), None, None),
        P(),
        P(),
        P(),
        P(),
        P(),
    )
    out_specs = P(None, None, "col", "kgrp", None, "row")
    return jax.shard_map(
        functools.partial(shards, sizes),
        mesh=mesh,
        in_specs=in_specs,
        out_specs=out_specs,
        check_vma=False,
    )
```

time: 205 us -> 68.5 us (0.33)
  the two profiles are of different devices: /device:TPU:16 before, /device:TPU:6 now
where the time goes in v1:
time: 68.5 us; the launch traced here: 68.2 us
  Pallas kernels  65.2 us (95%)
  local copies, waits for them, and re-layouts  2.33 us (3%)
    pallas_call x1, Pallas kernels, shards(): pl.pallas_call(functools.partial(kernel, sizes), out_shape=jax.ShapeDtype...  65.2 us
    broadcast_in_dim x1, local copies, waits for them, and re-layouts, shards(): return jnp.transpose(result, (0, 1, 3, 2, 4))[:, :, None]  1.39 us

profile of v1, /device:TPU:6, one launch (start us, length us, event | category | flops | bytes accessed | tf_op | source)
XLA Modules:
  0.0 68.2 jit_solution(1098630864466076653)
XLA Ops:
  0.0 0.0 copy-start
  0.0 0.9 %stack.9 = bf16[1,2,16,1024]{3,2,1,0:T(8,128)(2,1)S(1)} reshape(bf16[2,16,2,512]{3,2,1,0:T(2,128)(2,1)} %param.7) | data formatting | bytes 131072 | tf_op jit(solution)/shard_map/stack | solution.py:232
  0.9 0.0 copy-done
  1.0 0.7 pad_maximum_fusion.own_ref
  1.6 65.2 %polarizability.1 = f32[2,2,2,8,128]{4,3,2,1,0:T(8,128)} custom-call(bf16[2,2,16,1024]{3,2,1,0:T(8,128)(2,1)} %pad_maximum_fusion.own_ref, f32[2,32,512]{2,1,0:T(8,128)} %energies.1, s32[2,32,512]{2,1,0:T(8,128)} %band_order.1, f32[2]{0:T(128)} %imag_times.1, s32[2,32]{1,0:T(2,128)} %kq_map.1, s32[32]{0:T(128)} %slot_kpoint.1), custom_call_target="tpu_custom_call" | custom-call | tf_op jit(solution)/shard_map/polarizability/pallas_call | solution.py:235
  66.8 1.4 %copy.8 = f32[2,2,1,8,2,128]{5,4,3,2,1,0:T(2,128)} copy(f32[2,2,1,8,2,128]{5,3,4,1,0,2:T(8,128)} %bitcast.3) | data formatting | bytes 65536 | tf_op jit(solution)/shard_map/broadcast_in_dim | solution.py:259
  (1 shorter events, 0.0 us)
Async XLA Ops:
  0.0 0.9 %copy-start = (bf16[2,16,2,512]{3,2,1,0:T(2,128)(2,1)S(1)}, bf16[2,16,2,512]{3,2,1,0:T(2,128)(2,1)}, u32[]{:S(2)}) copy-start(bf16[2,16,2,512]{3,2,1,0:T(2,128)(2,1)} %param.8) | copy-start | bytes 196612

commit v2 on v1

v2 whole, which is shorter than its diff:
```python
import functools

import jax
import jax.numpy as jnp
from jax import lax
from jax.experimental import pallas as pl
from jax.experimental.pallas import tpu as pltpu
from jax.sharding import PartitionSpec as P

MESH = pl.DeviceIdType.MESH
CORES = 2
LANES = 128
NEAR = (2, -2, 1, -1)
TOP = 32767.0


def band_weights(levels, ranks, imag_times):
    pieces = levels.shape[1] // LANES
    picked = []
    for b in range(pieces):
        rank = ranks[:, b * LANES : (b + 1) * LANES]
        lane = rank % LANES
        found = jnp.zeros(rank.shape, jnp.float32)
        for c in range(pieces):
            taken = jnp.take_along_axis(levels[:, c * LANES : (c + 1) * LANES], lane, axis=1)
            found = jnp.where(rank // LANES == c, taken, found)
        picked.append(found)
    picked = jnp.concatenate(picked, axis=1)
    return [jnp.exp(-picked * imag_times[t]) for t in range(2)]


def kernel(
    sizes,
    occ_hbm,
    emp_hbm,
    energies_hbm,
    order_hbm,
    times_hbm,
    kq_hbm,
    kpoint_hbm,
    out_ref,
    raw,
    levels,
    ranks,
    rows,
    cols,
    packed,
    landed,
    decoded,
    imag_times,
    kq_map,
    slot_kpoint,
    inverse,
    row_send,
    row_recv,
    col_send,
    col_recv,
    mate_send,
    mate_recv,
    tile_send,
    tile_recv,
    local_sem,
):
    groups, row_count, col_count = sizes
    xs, line = groups // 2, row_count // CORES
    per_group = raw.shape[1]
    bands = raw.shape[4]
    kpoints = groups * per_group
    group, row, y = lax.axis_index("kgrp"), lax.axis_index("row"), lax.axis_index("col")
    x, zh = group // 2, group % 2
    zl, core = row // CORES, row % CORES

    def along_y(step):
        return (group, row, lax.rem(y + step + col_count, col_count))

    def along_z(step):
        return (group, lax.rem(zl + step, line) * CORES + core, y)

    mate = (group, zl * CORES + 1 - core, y)
    others = [(dx, dz) for dx in (4, 3, 5, 2, 6, 1, 7, 0) for dz in (1, 0) if dx or dz]

    def group_at(dx, dz):
        return lax.rem(x + dx, xs) * 2 + lax.rem(zh + dz, 2)

    peers = [(group_at(dx, dz), row, y) for dx, dz in others]
    peers += [along_z(e) for e in range(1, line)] + [along_y(s) for s in NEAR] + [mate]
    barrier = pltpu.get_barrier_semaphore()
    for peer in peers:
        pl.semaphore_signal(barrier, inc=1, device_id=peer, device_id_type=MESH)

    own = pl.ds(group * per_group, per_group)
    fetches = [
        pltpu.make_async_copy(occ_hbm, raw.at[0], local_sem.at[0]),
        pltpu.make_async_copy(emp_hbm, raw.at[1], local_sem.at[1]),
        pltpu.make_async_copy(times_hbm, imag_times, local_sem.at[2]),
        pltpu.make_async_copy(kq_hbm, kq_map, local_sem.at[3]),
        pltpu.make_async_copy(kpoint_hbm, slot_kpoint, local_sem.at[4]),
    ]
    for kind in range(2):
        part = pl.ds(kind * per_group, per_group)
        fetches += [
            pltpu.make_async_copy(
                energies_hbm.at[kind, own], levels.at[part], local_sem.at[5 + kind]
            ),
            pltpu.make_async_copy(order_hbm.at[kind, own], ranks.at[part], local_sem.at[7 + kind]),
        ]
    for copy in fetches:
        copy.start()
    for copy in fetches:
        copy.wait()
    for kind in range(2):
        for slot in range(per_group):
            for part in range(2):
                piece = raw[kind, slot, :, part, :]
                span = slice(part * bands, (part + 1) * bands)
                rows[kind, y, slot, :, span] = piece
                cols[kind, row, slot, :, span] = piece

    pl.semaphore_wait(barrier, len(peers))

    row_copies, col_copies, mate_copies, tile_copies = {}, {}, {}, {}

    def send_rows(kind, distance, step):
        source = lax.rem(y - (distance - step) + col_count, col_count)
        key = (kind, distance % col_count)
        row_copies[key] = pltpu.make_async_remote_copy(
            src_ref=rows.at[kind, source],
            dst_ref=rows.at[kind, source],
            send_sem=row_send.at[key[0], key[1]],
            recv_sem=row_recv.at[key[0], key[1]],
            device_id=along_y(step),
            device_id_type=MESH,
        )
        row_copies[key].start()

    def send_cols(kind, step):
        col_copies[kind, step] = pltpu.make_async_remote_copy(
            src_ref=cols.at[kind, row],
            dst_ref=cols.at[kind, row],
            send_sem=col_send.at[kind, step],
            recv_sem=col_recv.at[kind, step],
            device_id=along_z(step),
            device_id_type=MESH,
        )
        col_copies[kind, step].start()

    def send_mate(kind, step):
        source = lax.rem(zl - step + line, line) * CORES + core
        mate_copies[kind, step] = pltpu.make_async_remote_copy(
            src_ref=cols.at[kind, source],
            dst_ref=cols.at[kind, source],
            send_sem=mate_send.at[kind, step],
            recv_sem=mate_recv.at[kind, step],
            device_id=mate,
            device_id_type=MESH,
        )
        mate_copies[kind, step].start()

    for kind in range(2):
        for step in NEAR[:2]:
            send_rows(kind, step, step)
        for step in (2, 3, 1):
            send_cols(kind, step)
        for step in NEAR[2:]:
            send_rows(kind, step, step)
        send_mate(kind, 0)

    def find(k, carry):
        slot = jnp.int32(0)
        for s in range(kpoints):
            slot = jnp.where(slot_kpoint[s] == k, s, slot)
        inverse[k] = slot
        return carry

    lax.fori_loop(0, kpoints, find, 0)
    twice = [jnp.concatenate([ref[...], ref[...]], axis=0) for ref in (levels, ranks)]
    weights = band_weights(*twice, imag_times)

    for kind in range(2):
        for sign in (1, -1):
            row_copies[kind, 2 * sign % col_count].wait_recv()
            if (sign == 1) == (kind == 0):
                send_rows(kind, 4 * sign, 2 * sign)
            send_rows(kind, 3 * sign, sign)
        for step in (1, 2, 3):
            col_copies[kind, step].wait_recv()
            send_mate(kind, step)

    points = row_count * raw.shape[2]
    share = points // groups
    lanes = lax.broadcasted_iota(jnp.int32, (points, LANES), 1)
    for kind in range(2):
        for distance in (1, 7, 3, 5, 4):
            row_copies[kind, distance].wait_recv()
        for step in range(line):
            mate_copies[kind, step].wait_recv()
        powers = jnp.zeros((points, LANES), jnp.float32)
        for slot in range(per_group):
            row_panel = rows[kind, :, slot].reshape(-1, 2 * bands)
            col_panel = cols[kind, :, slot].reshape(-1, 2 * bands)
            at = kind * per_group + slot
            w = [weights[t][at : at + 1] for t in range(2)]
            wide = row_panel.astype(jnp.float32)
            scaled = jnp.concatenate(
                [wide * jnp.concatenate([w[t], w[t]], axis=1) for t in range(2)], axis=0
            ).astype(jnp.bfloat16)
            turned = jnp.concatenate([-col_panel[:, bands:], col_panel[:, :bands]], axis=1)
            stacked = jnp.concatenate([col_panel, turned], axis=0)
            tile = lax.dot_general(
                stacked, scaled, (((1,), (1,)), ((), ())), preferred_element_type=jnp.float32
            )
            for t in range(2):
                span = slice(t * LANES, (t + 1) * LANES)
                pair = [tile[:points, span], tile[points:, span]]
                largest = jnp.maximum(jnp.abs(pair[0]), jnp.abs(pair[1]))
                largest = jnp.maximum(jnp.max(largest, axis=1, keepdims=True), 1e-30)
                power = jnp.floor(jnp.log2(largest)) + 1.0
                unit = jnp.exp2(15.0 - power)
                powers = jnp.where(lanes == slot * 2 + t, power, powers)
                for comp in range(2):
                    value = jnp.clip(jnp.round(pair[comp] * unit), -TOP, TOP).astype(jnp.int16)
                    packed[kind, :, slot * 2 + t, comp * share : (comp + 1) * share] = (
                        value.reshape(groups, share, LANES)
                    )
        coded = powers.astype(jnp.int16).reshape(groups, share, LANES)
        for comp in range(2):
            packed[kind, :, 2 * per_group, comp * share : (comp + 1) * share] = coded
        for n, (dx, dz) in enumerate(others):
            there = group_at(dx, dz)
            tile_copies[kind, n] = pltpu.make_async_remote_copy(
                src_ref=packed.at[kind, there],
                dst_ref=landed.at[kind, group],
                send_sem=tile_send.at[kind, n],
                recv_sem=tile_recv.at[kind, n],
                device_id=(there, row, y),
                device_id_type=MESH,
            )
            tile_copies[kind, n].start()

    for copy in (*row_copies.values(), *col_copies.values(), *mate_copies.values()):
        copy.wait_send()

    def decode(kind, held, source):
        unit = jnp.exp2(held[kind, source, 2 * per_group].astype(jnp.float32) - 15.0)
        for slot in range(per_group):
            for t in range(2):
                k = slot * 2 + t
                value = held[kind, source, k].astype(jnp.float32) * unit[:, k : k + 1]
                decoded[kind, source * per_group + slot, t] = value

    for kind in range(2):
        decode(kind, packed, group)
        for n, (dx, dz) in reversed(list(enumerate(others))):
            tile_copies[kind, n].wait_recv()
            decode(kind, landed, group_at(-dx % xs, dz))

    def add(j, totals):
        held = decoded[0, j]
        held_re, held_im = held[:, :share], held[:, share:]
        kpoint = slot_kpoint[j]
        new = []
        for q in range(2):
            moved = decoded[1, inverse[kq_map[q, kpoint]]]
            moved_re, moved_im = moved[:, :share], moved[:, share:]
            new.append(totals[2 * q] + (held_re * moved_re + held_im * moved_im))
            new.append(totals[2 * q + 1] + (held_im * moved_re - held_re * moved_im))
        return tuple(new)

    zero = jnp.zeros((2, share, LANES), jnp.float32)
    totals = lax.fori_loop(0, kpoints, add, (zero,) * 4)
    for q in range(2):
        for comp in range(2):
            for t in range(2):
                out_ref[comp, q, 0, :, t, :] = totals[2 * q + comp][t] * (-1.0 / kpoints)
    for copy in tile_copies.values():
        copy.wait_send()


def shards(sizes, occ, emp, energies, band_order, imag_times, kq_map, slot_kpoint):
    groups, row_count, col_count = sizes
    per_group, chunk, parts, bands = occ.shape
    width = parts * bands
    share = row_count * chunk // groups
    kpoints = groups * per_group
    dma = pltpu.SemaphoreType.DMA
    return pl.pallas_call(
        functools.partial(kernel, sizes),
        out_shape=jax.ShapeDtypeStruct((2, 2, 1, share, 2, col_count * chunk), jnp.float32),
        in_specs=[pl.BlockSpec(memory_space=pl.ANY)] * 7,
        out_specs=pl.BlockSpec(memory_space=pltpu.VMEM),
        scratch_shapes=[
            pltpu.VMEM((2, *occ.shape), jnp.bfloat16),
            pltpu.VMEM((2 * per_group, bands), jnp.float32),
            pltpu.VMEM((2 * per_group, bands), jnp.int32),
            pltpu.VMEM((2, col_count, per_group, chunk, width), jnp.bfloat16),
            pltpu.VMEM((2, row_count, per_group, chunk, width), jnp.bfloat16),
            pltpu.VMEM((2, groups, 2 * per_group + 1, 2 * share, LANES), jnp.int16),
            pltpu.VMEM((2, groups, 2 * per_group + 1, 2 * share, LANES), jnp.int16),
            pltpu.VMEM((2, kpoints, 2, 2 * share, LANES), jnp.float32),
            pltpu.SMEM(imag_times.shape, jnp.float32),
            pltpu.SMEM(kq_map.shape, jnp.int32),
            pltpu.SMEM(slot_kpoint.shape, jnp.int32),
            pltpu.SMEM((kpoints,), jnp.int32),
            dma((2, col_count)),
            dma((2, col_count)),
            dma((2, 4)),
            dma((2, 4)),
            dma((2, 4)),
            dma((2, 4)),
            dma((2, groups)),
            dma((2, groups)),
            dma((9,)),
        ],
        compiler_params=pltpu.CompilerParams(collective_id=0, has_side_effects=True),
        name="polarizability",
    )(occ, emp, energies, band_order, imag_times, kq_map, slot_kpoint)


def solution(mesh):
    sizes = (mesh.shape["kgrp"], mesh.shape["row"], mesh.shape["col"])
    in_specs = (
        P("kgrp", ("row", "col"), None, None),
        P("kgrp", ("row", "col"), None, None),
        P(),
        P(),
        P(),
        P(),
        P(),
    )
    out_specs = P(None, None, "col", "kgrp", None, "row")
    return jax.shard_map(
        functools.partial(shards, sizes),
        mesh=mesh,
        in_specs=in_specs,
        out_specs=out_specs,
        check_vma=False,
    )
```

time: 68.5 us -> 58.9 us (0.86)
  Pallas kernels: 65.2 us -> 57.2 us
  local copies, waits for them, and re-layouts: 2.33 us -> 1.38 us
    pallas_call x1, Pallas kernels: 65.2 us -> 57.2 us  [shards(): pl.pallas_call(functools.partial(kernel, sizes), out_shape=jax.ShapeDtype...]
    broadcast_in_dim x1 -> x0, local copies, waits for them, and re-layouts: 1.39 us -> none  [shards(): return jnp.transpose(result, (0, 1, 3, 2, 4))[:, :, None]]
    unnamed x2 -> x1, local copies, waits for them, and re-layouts: 0.01 us -> 1.38 us
    another operation x2 -> x0, local copies, waits for them, and re-layouts: 0.94 us -> none  [shards(): own = jnp.stack([occ, emp]).reshape(2, per_group, chunk, width)]
where the time goes in v2:
time: 58.9 us; the launch traced here: 58.6 us
  Pallas kernels  57.2 us (97%)
  local copies, waits for them, and re-layouts  1.38 us (2%)
    pallas_call x1, Pallas kernels, shards(): pl.pallas_call(functools.partial(kernel, sizes), out_shape=jax.ShapeDtype...  57.2 us
    unnamed x1, local copies, waits for them, and re-layouts  1.38 us

profile of v2, /device:TPU:6, one launch (start us, length us, event | category | flops | bytes accessed | tf_op | source)
XLA Modules:
  0.0 58.6 jit_solution(10382115110784423357)
XLA Ops:
  0.0 57.2 %polarizability.1 = f32[2,2,1,8,2,128]{5,4,3,2,1,0:T(2,128)} custom-call(bf16[2,16,2,512]{3,2,1,0:T(2,128)(2,1)} %occ_hbm.1, bf16[2,16,2,512]{3,2,1,0:T(2,128)(2,1)} %emp_hbm.1, f32[2,32,512]{2,1,0:T(8,128)} %energies_hbm.1, s32[2,32,512]{2,1,0:T(8,128)} %order_hbm.1, f32[2]{0:T(128)} %times_hbm.1, s32[2,32]{1,0:T(2,128)} %kq_hbm.1, s32[32]{0:T(128)} %kpoint_hbm.1), custom_call_target="tpu_custom_call" | custom-call | tf_op jit(solution)/shard_map/polarizability/pallas_call | solution.py:286
  57.2 1.4 %copy.9 = f32[2,2,1,8,2,128]{5,4,3,2,1,0:T(2,128)} copy(f32[2,2,1,8,2,128]{5,4,3,2,1,0:T(2,128)} %polarizability.1) | data formatting | bytes 65536

commit v3 on v2

--- a/solution.py
+++ b/solution.py
@@ -12,6 +12,7 @@
 LANES = 128
 NEAR = (2, -2, 1, -1)
 TOP = 32767.0
+RELAY = ((1, -1), (2, -2), (1, -1))
 
 
 def band_weights(levels, ranks, imag_times):
@@ -60,6 +61,7 @@
     tile_send,
     tile_recv,
     local_sem,
+    relay_sem,
 ):
     groups, row_count, col_count = sizes
     xs, line = groups // 2, row_count // CORES
@@ -82,7 +84,10 @@
     def group_at(dx, dz):
         return lax.rem(x + dx, xs) * 2 + lax.rem(zh + dz, 2)
 
-    peers = [(group_at(dx, dz), row, y) for dx, dz in others]
+    def along_x(dx, dz=0):
+        return (group_at(dx % xs, dz), row, y)
+
+    peers = [along_x(0, 1), along_x(1), along_x(-1)]
     peers += [along_z(e) for e in range(1, line)] + [along_y(s) for s in NEAR] + [mate]
     barrier = pltpu.get_barrier_semaphore()
     for peer in peers:
@@ -118,6 +123,17 @@
 
     pl.semaphore_wait(barrier, len(peers))
 
+    def relay(stage):
+        if stage:
+            pl.semaphore_wait(relay_sem.at[stage - 1], len(RELAY[stage - 1]))
+        if stage < len(RELAY):
+            for dx in RELAY[stage]:
+                pl.semaphore_signal(
+                    relay_sem.at[stage], inc=1, device_id=along_x(dx), device_id_type=MESH
+                )
+
+    relay(0)
+
     row_copies, col_copies, mate_copies, tile_copies = {}, {}, {}, {}
 
     def send_rows(kind, distance, step):
@@ -156,7 +172,7 @@
         )
         mate_copies[kind, step].start()
 
-    for kind in range(2):
+    def first_leg(kind):
         for step in NEAR[:2]:
             send_rows(kind, step, step)
         for step in (2, 3, 1):
@@ -165,6 +181,20 @@
             send_rows(kind, step, step)
         send_mate(kind, 0)
 
+    def second_leg(kind):
+        for sign in (1, -1):
+            row_copies[kind, 2 * sign % col_count].wait_recv()
+            if (sign == 1) == (kind == 0):
+                send_rows(kind, 4 * sign, 2 * sign)
+            send_rows(kind, 3 * sign, sign)
+
+    def hand_over(kind):
+        for step in (1, 2, 3):
+            col_copies[kind, step].wait_recv()
+            send_mate(kind, step)
+
+    first_leg(0)
+
     def find(k, carry):
         slot = jnp.int32(0)
         for s in range(kpoints):
@@ -176,20 +206,20 @@
     twice = [jnp.concatenate([ref[...], ref[...]], axis=0) for ref in (levels, ranks)]
     weights = band_weights(*twice, imag_times)
 
-    for kind in range(2):
-        for sign in (1, -1):
-            row_copies[kind, 2 * sign % col_count].wait_recv()
-            if (sign == 1) == (kind == 0):
-                send_rows(kind, 4 * sign, 2 * sign)
-            send_rows(kind, 3 * sign, sign)
-        for step in (1, 2, 3):
-            col_copies[kind, step].wait_recv()
-            send_mate(kind, step)
+    second_leg(0)
+    first_leg(1)
+    relay(1)
+    hand_over(0)
+    relay(2)
+    relay(3)
 
     points = row_count * raw.shape[2]
     share = points // groups
     lanes = lax.broadcasted_iota(jnp.int32, (points, LANES), 1)
     for kind in range(2):
+        if kind:
+            second_leg(kind)
+            hand_over(kind)
         for distance in (1, 7, 3, 5, 4):
             row_copies[kind, distance].wait_recv()
         for step in range(line):
@@ -271,7 +301,7 @@
     for q in range(2):
         for comp in range(2):
             for t in range(2):
-                out_ref[comp, q, 0, :, t, :] = totals[2 * q + comp][t] * (-1.0 / kpoints)
+                out_ref[comp, q, 0, :, t, :] = totals[2 * q + comp][t]
     for copy in tile_copies.values():
         copy.wait_send()
 
@@ -283,7 +313,7 @@
     share = row_count * chunk // groups
     kpoints = groups * per_group
     dma = pltpu.SemaphoreType.DMA
-    return pl.pallas_call(
+    totals = pl.pallas_call(
         functools.partial(kernel, sizes),
         out_shape=jax.ShapeDtypeStruct((2, 2, 1, share, 2, col_count * chunk), jnp.float32),
         in_specs=[pl.BlockSpec(memory_space=pl.ANY)] * 7,
@@ -310,10 +340,12 @@
             dma((2, groups)),
             dma((2, groups)),
             dma((9,)),
+            pltpu.SemaphoreType.REGULAR((len(RELAY),)),
         ],
         compiler_params=pltpu.CompilerParams(collective_id=0, has_side_effects=True),
         name="polarizability",
     )(occ, emp, energies, band_order, imag_times, kq_map, slot_kpoint)
+    return totals * (-1.0 / kpoints)
 
 
 def solution(mesh):

time: 58.9 us -> 54.7 us (0.929)
  Pallas kernels: 57.2 us -> 53 us
  other arithmetic: 0 us -> 1.39 us
  local copies, waits for them, and re-layouts: 1.38 us -> 0 us
    pallas_call x1, Pallas kernels: 57.2 us -> 53 us  [shards(): pl.pallas_call(functools.partial(kernel, sizes), out_shape=jax.ShapeDtype...]
    mul x0 -> x1, other arithmetic: none -> 1.39 us  [shards(): return totals * (-1.0 / kpoints)]
    unnamed x1 -> x0, local copies, waits for them, and re-layouts: 1.38 us -> none
where the time goes in v3:
time: 54.7 us; the launch traced here: 54.4 us
  Pallas kernels  53 us (97%)
  other arithmetic  1.39 us (3%)
    pallas_call x1, Pallas kernels, shards(): pl.pallas_call(functools.partial(kernel, sizes), out_shape=jax.ShapeDtype...  53 us
    mul x1, other arithmetic, shards(): return totals * (-1.0 / kpoints)  1.39 us

profile of v3, /device:TPU:6, one launch (start us, length us, event | category | flops | bytes accessed | tf_op | source)
XLA Modules:
  0.0 54.4 jit_solution(13266098825823067135)
XLA Ops:
  0.0 53.0 %polarizability.1 = f32[2,2,1,8,2,128]{5,4,3,2,1,0:T(2,128)} custom-call(bf16[2,16,2,512]{3,2,1,0:T(2,128)(2,1)} %occ_hbm.1, bf16[2,16,2,512]{3,2,1,0:T(2,128)(2,1)} %emp_hbm.1, f32[2,32,512]{2,1,0:T(8,128)} %energies_hbm.1, s32[2,32,512]{2,1,0:T(8,128)} %order_hbm.1, f32[2]{0:T(128)} %times_hbm.1, s32[2,32]{1,0:T(2,128)} %kq_hbm.1, s32[32]{0:T(128)} %kpoint_hbm.1), custom_call_target="tpu_custom_call" | custom-call | tf_op jit(solution)/shard_map/polarizability/pallas_call | solution.py:316
  53.0 1.4 %broadcast_multiply_fusion = f32[2,2,1,8,2,128]{5,4,3,2,1,0:T(2,128)} fusion(f32[2,2,1,8,2,128]{5,4,3,2,1,0:T(2,128)} %polarizability.1), kind=kLoop, calls=%fused_computation | loop fusion | flops 8192 | bytes 65536 | tf_op jit(solution)/shard_map/mul | solution.py:348

commit v4 on v3

--- a/solution.py
+++ b/solution.py
@@ -216,6 +216,7 @@
     points = row_count * raw.shape[2]
     share = points // groups
     lanes = lax.broadcasted_iota(jnp.int32, (points, LANES), 1)
+    powers = jnp.zeros((points, LANES), jnp.float32)
     for kind in range(2):
         if kind:
             second_leg(kind)
@@ -224,7 +225,6 @@
             row_copies[kind, distance].wait_recv()
         for step in range(line):
             mate_copies[kind, step].wait_recv()
-        powers = jnp.zeros((points, LANES), jnp.float32)
         for slot in range(per_group):
             row_panel = rows[kind, :, slot].reshape(-1, 2 * bands)
             col_panel = cols[kind, :, slot].reshape(-1, 2 * bands)
@@ -246,20 +246,23 @@
                 largest = jnp.maximum(jnp.max(largest, axis=1, keepdims=True), 1e-30)
                 power = jnp.floor(jnp.log2(largest)) + 1.0
                 unit = jnp.exp2(15.0 - power)
-                powers = jnp.where(lanes == slot * 2 + t, power, powers)
+                powers = jnp.where(lanes == at * 2 + t, power, powers)
                 for comp in range(2):
                     value = jnp.clip(jnp.round(pair[comp] * unit), -TOP, TOP).astype(jnp.int16)
                     packed[kind, :, slot * 2 + t, comp * share : (comp + 1) * share] = (
                         value.reshape(groups, share, LANES)
                     )
-        coded = powers.astype(jnp.int16).reshape(groups, share, LANES)
-        for comp in range(2):
-            packed[kind, :, 2 * per_group, comp * share : (comp + 1) * share] = coded
+        count = 2 * per_group + kind
+        if kind:
+            coded = powers.astype(jnp.int16).reshape(groups, share, LANES)
+            for comp in range(2):
+                span = slice(comp * share, (comp + 1) * share)
+                packed[kind, :, 2 * per_group, span] = coded
         for n, (dx, dz) in enumerate(others):
             there = group_at(dx, dz)
             tile_copies[kind, n] = pltpu.make_async_remote_copy(
-                src_ref=packed.at[kind, there],
-                dst_ref=landed.at[kind, group],
+                src_ref=packed.at[kind, there, pl.ds(0, count)],
+                dst_ref=landed.at[kind, group, pl.ds(0, count)],
                 send_sem=tile_send.at[kind, n],
                 recv_sem=tile_recv.at[kind, n],
                 device_id=(there, row, y),
@@ -270,19 +273,21 @@
     for copy in (*row_copies.values(), *col_copies.values(), *mate_copies.values()):
         copy.wait_send()
 
-    def decode(kind, held, source):
-        unit = jnp.exp2(held[kind, source, 2 * per_group].astype(jnp.float32) - 15.0)
-        for slot in range(per_group):
-            for t in range(2):
-                k = slot * 2 + t
-                value = held[kind, source, k].astype(jnp.float32) * unit[:, k : k + 1]
-                decoded[kind, source * per_group + slot, t] = value
-
-    for kind in range(2):
-        decode(kind, packed, group)
-        for n, (dx, dz) in reversed(list(enumerate(others))):
+    def decode(held, source):
+        unit = jnp.exp2(held[1, source, 2 * per_group].astype(jnp.float32) - 15.0)
+        for kind in range(2):
+            for slot in range(per_group):
+                for t in range(2):
+                    k = slot * 2 + t
+                    at = kind * per_group * 2 + k
+                    value = held[kind, source, k].astype(jnp.float32) * unit[:, at : at + 1]
+                    decoded[kind, source * per_group + slot, t] = value
+
+    decode(packed, group)
+    for n, (dx, dz) in reversed(list(enumerate(others))):
+        for kind in range(2):
             tile_copies[kind, n].wait_recv()
-            decode(kind, landed, group_at(-dx % xs, dz))
+        decode(landed, group_at(-dx % xs, dz))
 
     def add(j, totals):
         held = decoded[0, j]
@@ -315,7 +320,7 @@
     dma = pltpu.SemaphoreType.DMA
     totals = pl.pallas_call(
         functools.partial(kernel, sizes),
-        out_shape=jax.ShapeDtypeStruct((2, 2, 1, share, 2, col_count * chunk), jnp.float32),
+        out_shape=pltpu.VMEM((2, 2, 1, share, 2, col_count * chunk), jnp.float32),
         in_specs=[pl.BlockSpec(memory_space=pl.ANY)] * 7,
         out_specs=pl.BlockSpec(memory_space=pltpu.VMEM),
         scratch_shapes=[

time: 54.7 us -> 52.8 us (0.965)
  Pallas kernels: 53 us -> 51.9 us
  other arithmetic: 1.39 us -> 0.63 us
    pallas_call x1, Pallas kernels: 53 us -> 51.9 us  [shards(): pl.pallas_call(functools.partial(kernel, sizes), out_shape=pltpu.VMEM((2,...]
    mul x1, other arithmetic: 1.39 us -> 0.63 us  [shards(): return totals * (-1.0 / kpoints)]
where the time goes in v4:
time: 52.8 us; the launch traced here: 52.6 us
  Pallas kernels  51.9 us (98%)
  other arithmetic  0.63 us (1%)
    pallas_call x1, Pallas kernels, shards(): pl.pallas_call(functools.partial(kernel, sizes), out_shape=pltpu.VMEM((2,...  51.9 us

profile of v4, /device:TPU:6, one launch (start us, length us, event | category | flops | bytes accessed | tf_op | source)
XLA Modules:
  0.0 52.6 jit_solution(18105038179570803268)
XLA Ops:
  0.0 51.9 %polarizability.1 = f32[2,2,1,8,2,128]{5,4,3,2,1,0:T(2,128)S(1)} custom-call(bf16[2,16,2,512]{3,2,1,0:T(2,128)(2,1)} %occ_hbm.1, bf16[2,16,2,512]{3,2,1,0:T(2,128)(2,1)} %emp_hbm.1, f32[2,32,512]{2,1,0:T(8,128)} %energies_hbm.1, s32[2,32,512]{2,1,0:T(8,128)} %order_hbm.1, f32[2]{0:T(128)} %times_hbm.1, s32[2,32]{1,0:T(2,128)} %kq_hbm.1, s32[32]{0:T(128)} %kpoint_hbm.1), custom_call_target="tpu_custom_call" | custom-call | tf_op jit(solution)/shard_map/polarizability/pallas_call | solution.py:321
  51.9 0.6 %broadcast_multiply_fusion = f32[2,2,1,8,2,128]{5,4,3,2,1,0:T(2,128)} fusion(f32[2,2,1,8,2,128]{5,4,3,2,1,0:T(2,128)S(1)} %polarizability.1), kind=kLoop, calls=%fused_computation | loop fusion | flops 8192 | bytes 65536 | tf_op jit(solution)/shard_map/mul | solution.py:353

commit v5 on v4

--- a/solution.py
+++ b/solution.py
@@ -10,6 +10,7 @@
 MESH = pl.DeviceIdType.MESH
 CORES = 2
 LANES = 128
+UNROLL = 4
 NEAR = (2, -2, 1, -1)
 TOP = 32767.0
 RELAY = ((1, -1), (2, -2), (1, -1))
@@ -52,6 +53,7 @@
     kq_map,
     slot_kpoint,
     inverse,
+    sources,
     row_send,
     row_recv,
     col_send,
@@ -121,6 +123,9 @@
                 rows[kind, y, slot, :, span] = piece
                 cols[kind, row, slot, :, span] = piece
 
+    twice = [jnp.concatenate([ref[...], ref[...]], axis=0) for ref in (levels, ranks)]
+    weights = band_weights(*twice, imag_times)
+
     pl.semaphore_wait(barrier, len(peers))
 
     def relay(stage):
@@ -202,9 +207,12 @@
         inverse[k] = slot
         return carry
 
+    def look_up(j, carry):
+        for q in range(2):
+            sources[q, j] = inverse[kq_map[q, slot_kpoint[j]]]
+        return carry
+
     lax.fori_loop(0, kpoints, find, 0)
-    twice = [jnp.concatenate([ref[...], ref[...]], axis=0) for ref in (levels, ranks)]
-    weights = band_weights(*twice, imag_times)
 
     second_leg(0)
     first_leg(1)
@@ -273,6 +281,8 @@
     for copy in (*row_copies.values(), *col_copies.values(), *mate_copies.values()):
         copy.wait_send()
 
+    lax.fori_loop(0, kpoints, look_up, 0)
+
     def decode(held, source):
         unit = jnp.exp2(held[1, source, 2 * per_group].astype(jnp.float32) - 15.0)
         for kind in range(2):
@@ -289,20 +299,22 @@
             tile_copies[kind, n].wait_recv()
         decode(landed, group_at(-dx % xs, dz))
 
-    def add(j, totals):
-        held = decoded[0, j]
-        held_re, held_im = held[:, :share], held[:, share:]
-        kpoint = slot_kpoint[j]
-        new = []
-        for q in range(2):
-            moved = decoded[1, inverse[kq_map[q, kpoint]]]
-            moved_re, moved_im = moved[:, :share], moved[:, share:]
-            new.append(totals[2 * q] + (held_re * moved_re + held_im * moved_im))
-            new.append(totals[2 * q + 1] + (held_im * moved_re - held_re * moved_im))
-        return tuple(new)
+    def add(step, totals):
+        for part in range(UNROLL):
+            j = step * UNROLL + part
+            held = decoded[0, j]
+            held_re, held_im = held[:, :share], held[:, share:]
+            new = []
+            for q in range(2):
+                moved = decoded[1, sources[q, j]]
+                moved_re, moved_im = moved[:, :share], moved[:, share:]
+                new.append(totals[2 * q] + (held_re * moved_re + held_im * moved_im))
+                new.append(totals[2 * q + 1] + (held_im * moved_re - held_re * moved_im))
+            totals = tuple(new)
+        return totals
 
     zero = jnp.zeros((2, share, LANES), jnp.float32)
-    totals = lax.fori_loop(0, kpoints, add, (zero,) * 4)
+    totals = lax.fori_loop(0, kpoints // UNROLL, add, (zero,) * 4)
     for q in range(2):
         for comp in range(2):
             for t in range(2):
@@ -336,6 +348,7 @@
             pltpu.SMEM(kq_map.shape, jnp.int32),
             pltpu.SMEM(slot_kpoint.shape, jnp.int32),
             pltpu.SMEM((kpoints,), jnp.int32),
+            pltpu.SMEM((2, kpoints), jnp.int32),
             dma((2, col_count)),
             dma((2, col_count)),
             dma((2, 4)),

time: 52.8 us -> 52.4 us (level)
  no operation moved by 1% of the time
where the time goes in v5:
time: 52.4 us; the launch traced here: 52.2 us
  Pallas kernels  51.5 us (98%)
  other arithmetic  0.63 us (1%)
    pallas_call x1, Pallas kernels, shards(): pl.pallas_call(functools.partial(kernel, sizes), out_shape=pltpu.VMEM((2,...  51.5 us

profile of v5, /device:TPU:6, one launch (start us, length us, event | category | flops | bytes accessed | tf_op | source)
XLA Modules:
  0.0 52.2 jit_solution(15331957949214412157)
XLA Ops:
  0.0 51.5 %polarizability.1 = f32[2,2,1,8,2,128]{5,4,3,2,1,0:T(2,128)S(1)} custom-call(bf16[2,16,2,512]{3,2,1,0:T(2,128)(2,1)} %occ_hbm.1, bf16[2,16,2,512]{3,2,1,0:T(2,128)(2,1)} %emp_hbm.1, f32[2,32,512]{2,1,0:T(8,128)} %energies_hbm.1, s32[2,32,512]{2,1,0:T(8,128)} %order_hbm.1, f32[2]{0:T(128)} %times_hbm.1, s32[2,32]{1,0:T(2,128)} %kq_hbm.1, s32[32]{0:T(128)} %kpoint_hbm.1), custom_call_target="tpu_custom_call" | custom-call | tf_op jit(solution)/shard_map/polarizability/pallas_call | solution.py:333
  51.5 0.6 %broadcast_multiply_fusion = f32[2,2,1,8,2,128]{5,4,3,2,1,0:T(2,128)} fusion(f32[2,2,1,8,2,128]{5,4,3,2,1,0:T(2,128)S(1)} %polarizability.1), kind=kLoop, calls=%fused_computation | loop fusion | flops 8192 | bytes 65536 | tf_op jit(solution)/shard_map/mul | solution.py:366

commit v6 on v5

--- a/solution.py
+++ b/solution.py
@@ -154,6 +154,19 @@
         )
         row_copies[key].start()
 
+    def send_half(kind, sign):
+        source = lax.rem(y - 2 * sign + col_count, col_count)
+        slot, at = (0, 4) if sign == 1 else (1, 0)
+        row_copies[kind, at] = pltpu.make_async_remote_copy(
+            src_ref=rows.at[kind, source, slot],
+            dst_ref=rows.at[kind, source, slot],
+            send_sem=row_send.at[kind, at],
+            recv_sem=row_recv.at[kind, at],
+            device_id=along_y(2 * sign),
+            device_id_type=MESH,
+        )
+        row_copies[kind, at].start()
+
     def send_cols(kind, step):
         col_copies[kind, step] = pltpu.make_async_remote_copy(
             src_ref=cols.at[kind, row],
@@ -189,9 +202,8 @@
     def second_leg(kind):
         for sign in (1, -1):
             row_copies[kind, 2 * sign % col_count].wait_recv()
-            if (sign == 1) == (kind == 0):
-                send_rows(kind, 4 * sign, 2 * sign)
             send_rows(kind, 3 * sign, sign)
+            send_half(kind, sign)
 
     def hand_over(kind):
         for step in (1, 2, 3):
@@ -229,7 +241,7 @@
         if kind:
             second_leg(kind)
             hand_over(kind)
-        for distance in (1, 7, 3, 5, 4):
+        for distance in (1, 7, 3, 5, 4, 0):
             row_copies[kind, distance].wait_recv()
         for step in range(line):
             mate_copies[kind, step].wait_recv()

time: 52.4 us -> 52.1 us (level)
  no operation moved by 1% of the time
where the time goes in v6:
time: 52.1 us; the launch traced here: 51.9 us
  Pallas kernels  51.2 us (98%)
  other arithmetic  0.63 us (1%)
    pallas_call x1, Pallas kernels, shards(): pl.pallas_call(functools.partial(kernel, sizes), out_shape=pltpu.VMEM((2,...  51.2 us

profile of v6, /device:TPU:6, one launch (start us, length us, event | category | flops | bytes accessed | tf_op | source)
XLA Modules:
  0.0 51.9 jit_solution(11421561725316523761)
XLA Ops:
  0.0 51.2 %polarizability.1 = f32[2,2,1,8,2,128]{5,4,3,2,1,0:T(2,128)S(1)} custom-call(bf16[2,16,2,512]{3,2,1,0:T(2,128)(2,1)} %occ_hbm.1, bf16[2,16,2,512]{3,2,1,0:T(2,128)(2,1)} %emp_hbm.1, f32[2,32,512]{2,1,0:T(8,128)} %energies_hbm.1, s32[2,32,512]{2,1,0:T(8,128)} %order_hbm.1, f32[2]{0:T(128)} %times_hbm.1, s32[2,32]{1,0:T(2,128)} %kq_hbm.1, s32[32]{0:T(128)} %kpoint_hbm.1), custom_call_target="tpu_custom_call" | custom-call | tf_op jit(solution)/shard_map/polarizability/pallas_call | solution.py:345
  51.2 0.6 %broadcast_multiply_fusion = f32[2,2,1,8,2,128]{5,4,3,2,1,0:T(2,128)} fusion(f32[2,2,1,8,2,128]{5,4,3,2,1,0:T(2,128)S(1)} %polarizability.1), kind=kLoop, calls=%fused_computation | loop fusion | flops 8192 | bytes 65536 | tf_op jit(solution)/shard_map/mul | solution.py:378
